TPU v7x, 32 devices: a whole 2x2x4 slice. The times are simulated.
32 devices in a mesh: blk: 4 (over x, core), grp: 8 (over z, y).
Axes of the slice: x: 2, y: 2, z: 4, core: 2. Of those that a mesh axis runs over, the one named last changes fastest.
Arguments:
- amps: bfloat16 [1024, 2, 512], P(('blk', 'grp')), may hold values from -6 to 6
- domains: int32 [1024, 2], replicated, may hold values from 0 to 3, all different within a row
- owner: int32 [1024], replicated, may hold values from 0 to 1023, as said below
- coupling: int32 [4, 4], replicated, may hold values from 0 to 1, as said below
- integrals: bfloat16 [2048, 2048], P('blk', 'grp'), may hold values from -0.25 to 0.25
Outputs:
- residual: float32 [1024, 2048], P('blk', 'grp')
Inputs may be any that keep to these rules, and one draw needn't show every extreme that they name: `domains`: each row names 2 different pair blocks, and every block is named by some row. owner maps the occupied pairs of each group of 256 consecutive pairs one to one onto the slots of the same group. Every column of coupling holds exactly 2 ones.
All inputs are finite; a program needn't handle non-finite values.
Results may differ from a plain program's by a relative error of at most 0.0003.
Values may be sent and summed in bfloat16 or wider, within the bound.
A program may use at most 64 MiB of HBM per device.

v0:
```python
import jax
import jax.numpy as jnp
from jax import lax
from jax.sharding import PartitionSpec as P


def on_device(amps, domains, owner, coupling, integrals):
    n_blk = lax.axis_size("blk")
    me_blk = lax.axis_index("blk")
    me_grp = lax.axis_index("grp")
    block_rows, col_count = integrals.shape
    col_split = block_rows // col_count
    nvb = coupling.shape[0]
    op_total = owner.shape[0]
    op_grp = op_total // n_blk
    dom_width = domains.shape[1]
    target = me_grp // col_split
    blocks = jnp.arange(nvb, dtype=jnp.int32)
    keep_col = lax.dynamic_index_in_dim(coupling, target, axis=1, keepdims=False)
    group_base = me_blk * op_grp
    own_pairs = lax.dynamic_slice_in_dim(owner, group_base, op_grp)
    local_slots = own_pairs - group_base
    group_dom = lax.dynamic_slice_in_dim(domains, group_base, op_grp)
    permuter = (local_slots[:, None] == jnp.arange(op_grp, dtype=jnp.int32)[None, :]).astype(
        jnp.float32
    )
    pair_dom = jnp.dot(
        permuter, group_dom.astype(jnp.float32), precision=lax.Precision.HIGHEST
    ).astype(jnp.int32)
    in_domain = jnp.any(pair_dom == target, axis=1).astype(jnp.float32)
    group_amps = lax.all_gather(amps, "grp", axis=0, tiled=True)
    flat_amps = group_amps.reshape(op_grp, dom_width * block_rows)
    ordered = jnp.take(flat_amps, local_slots, axis=0).reshape(op_grp, dom_width, block_rows)
    selector = (pair_dom[:, :, None] == blocks[None, None, :]) & (keep_col[None, None, :] > 0)
    tile_full = jnp.einsum(
        "pkc,pkx->pcx", selector.astype(jnp.bfloat16), ordered, preferred_element_type=jnp.float32
    )
    tile_full = tile_full.astype(jnp.bfloat16).reshape(op_grp, nvb * block_rows)
    summed = jnp.dot(
        tile_full,
        lax.all_gather(integrals, "blk", axis=0, tiled=True),
        preferred_element_type=jnp.float32,
    )
    return summed * in_domain[:, None]


def solution(mesh):
    return jax.shard_map(
        on_device,
        mesh=mesh,
        in_specs=(P(("blk", "grp"), None, None), P(), P(), P(), P("blk", "grp")),
        out_specs=P("blk", "grp"),
        check_vma=False,
    )
```

profile of v0, /device:TPU:0, one launch (start us, length us, event | category | flops | bytes accessed | tf_op | source)
XLA Modules:
  0.0 56.2 jit_solution(8497213383912992596)
XLA Ops:
  6.5 0.0 all-gather.2.cloned.1.call-start
  6.5 0.7 %all-gather.2.cloned.1.call-update = ((bf16[512,256]{1,0:T(8,128)(2,1)}), bf16[2048,256]{1,0:T(8,128)(2,1)}) async-update(((), (), s32[]{:S(2)}) %all-gather.2.cloned.1.call-start, bf16[512,256]{1,0:T(8,128)(2,1)} %param.9) | async-update | bytes 1572888
  7.3 0.8 %compare_and_fusion = (pred[256]{0:T(512)(128)(4,1)S(1)}, s32[256]{0:T(256)S(1)}) fusion(s32[]{:T(128)S(6)} %mul.11, s32[1024]{0:T(1024)} %param.7, s32[]{:T(128)S(6)} %select_n.23), kind=kLoop, calls=%fused_computation.20 | loop fusion | flops 1792 | bytes 2312 | tf_op jit(solution)/shard_map/jit(_take)/and | solution.py:33
  8.0 1.0 %compare_reduce_fusion = (pred[256]{0:T(512)(128)(4,1)S(1)}, s32[256,2]{0,1:T(2,128)S(1)}) fusion(s32[]{:T(128)S(6)} %select_n.24, s32[1024,2]{0,1:T(2,128)} %param.6, s32[]{:T(128)S(6)} %select_n.23, s32[256]{0:T(256)S(1)} %get-tuple-element.6), kind=kOutput, calls=%fused_computation.14 | convolution fusion | flops 1640192 | bytes 5384 | tf_op jit(solution)/shard_map/dot_general | solution.py:27
  9.1 0.1 copy.7
  9.2 33.3 %all_gather.6 = bf16[256,2,512]{2,1,0:T(2,128)(2,1)S(1)} all-gather(bf16[32,2,512]{2,1,0:T(2,128)(2,1)} %param.5), channel_id=1, replica_groups=mesh['blk'=4,'grp'=8] {'grp'}, dimensions={0}, use_global_device_ids=true | all-gather | bytes 589824 | tf_op jit(solution)/shard_map/all_gather | solution.py:31
  42.5 0.1 copy.8
  42.6 1.2 %gather_fusion = bf16[256,1024]{1,0:T(8,128)(2,1)S(1)} fusion(bf16[256,1024]{1,0:T(8,128)(2,1)S(1)} %bitcast.6, s32[1024]{0:T(1024)S(1)} %pad_clamp_fusion), kind=kCustom, calls=%fused_computation | custom fusion | bytes 1049600 | tf_op jit(solution)/shard_map/jit(_take)/gather | solution.py:33
  43.8 0.0 copy-start
  43.8 0.4 gather.7
  44.2 0.3 copy-done
  44.4 0.2 fusion.9
  44.6 2.1 %convolution_convert_fusion = bf16[256,4,512]{2,1,0:T(4,128)(2,1)S(1)} fusion(bf16[256,2,512]{2,1,0:T(2,128)(2,1)S(1)} %gather.7, pred[256]{0:T(512)(128)(4,1)S(1)} %get-tuple-element.5, pred[4]{0:T(512)(128)(4,1)S(1)} %fusion.9, s32[256,2]{1,0:T(8,128)S(1)} %copy.7), kind=kOutput, calls=%fused_computation.1 | convolution fusion | flops 2887680 | bytes 1575172 | tf_op jit(solution)/shard_map/pkc,pkx->pcx/dot_general | solution.py:35
  46.7 0.3 copy.9
  47.0 0.0 all-gather.2.cloned.1.call-done
  47.0 2.4 %convolution_multiply_fusion = f32[256,256]{1,0:T(8,128)} fusion(bf16[256,2048]{1,0:T(8,128)(2,1)S(1)} %bitcast.7, bf16[2048,256]{1,0:T(8,128)(2,1)} %all-gather.2.cloned.1.call-done, f32[256]{0:T(256)S(1)} %convert_element_type.21), kind=kOutput, calls=%fused_computation.2 | convolution fusion | flops 268500992 | bytes 2360320 | tf_op jit(solution)/shard_map/dot_general | solution.py:39
  (3 shorter events, 0.0 us)
Async XLA Ops:
  6.5 40.5 %all-gather.2.cloned.1.call-start = ((), (), s32[]{:S(2)}) async-start(), calls=%async_computation | async-start | bytes 1310720 | tf_op jit(solution)/shard_map/all_gather | solution.py:41
  43.8 0.7 %copy-start = (s32[4,4]{1,0:T(4,128)S(1)}, s32[4,4]{1,0:T(4,128)}, u32[]{:S(2)}) copy-start(s32[4,4]{1,0:T(4,128)} %param.8) | copy-start | bytes 196
Sparse Core Ops, SparseCore 0:
  8.9 19.4 all-gather.1
where the time goes:
time: 56.4 us; the launch traced here: 56.2 us
  blocking collectives  33.3 us (59%)
  between operations  13.5 us (24%)
  matrix products  5.44 us (10%)
  local copies, waits for them, and re-layouts  2.3 us (4%)
  other arithmetic  0.98 us (2%)
  waiting for transfers between devices  0.73 us (1%)
    all_gather x1, blocking collectives, on_device(): group_amps = lax.all_gather(amps, 'grp', axis=0, tiled=True)  33.3 us
    dot_general x1, matrix products, on_device(): jnp.dot(tile_full, lax.all_gather(integrals, 'blk', axis=0, tiled=True),...  2.37 us
    dot_general x1, matrix products, on_device(): jnp.einsum('pkc,pkx->pcx', selector.astype(jnp.bfloat16), ordered, prefer...  2.05 us
    gather x2, local copies, waits for them, and re-layouts, on_device(): jnp.take(flat_amps, local_slots, axis=0)  1.54 us
  transfers between devices with their start and end apart: 1, of which 0 were waited for; matrix products, arithmetic and copies ran while one was open for 11% of the time, Pallas kernels for 0%

commit v1 on v0

v1 whole, which is shorter than its diff:
```python
import functools

import jax
import jax.numpy as jnp
from jax import lax
from jax.experimental import pallas as pl
from jax.experimental.pallas import tpu as pltpu
from jax.sharding import PartitionSpec as P

MESH = pl.DeviceIdType.MESH
F32 = jnp.float32
BF16 = jnp.bfloat16


def kernel(
    n_blk, n_grp, pieces,
    amps_ref, dom_ref, owner_ref, coupling_ref, ints_ref, out_ref,
    amp_buf, int_buf, tile_buf, code_buf,
    amp_z_send, amp_z_recv, amp_y_send, amp_y_recv,
    int_x_send, int_x_recv, int_c_send, int_c_recv, local_sem,
):
    chips, planes = n_blk // 2, n_grp // 2
    blk, grp = lax.axis_index("blk"), lax.axis_index("grp")
    x, core = blk // 2, blk % 2
    z, y = grp // 2, grp % 2
    slots, width, depth = amps_ref.shape
    rows = slots * width
    cols = ints_ref.shape[1]
    group = slots * n_grp
    nvb = n_blk
    target = grp // (depth // cols)
    cut = depth // pieces

    def at(b, g):
        return (b, g)

    mine = amp_buf.at[pl.ds(pl.multiple_of(grp * rows, rows), rows)]
    mine[...] = amps_ref[...].astype(F32).reshape(rows, depth).astype(BF16)

    peers = [at(blk, ((z + d) % planes) * 2 + y) for d in range(1, planes)]
    peers.append(at(blk, z * 2 + 1 - y))
    peers += [at(((x + d) % chips) * 2 + core, grp) for d in range(1, chips)]
    peers.append(at(x * 2 + 1 - core, grp))
    barrier = pltpu.get_barrier_semaphore()
    for peer in peers:
        pl.semaphore_signal(barrier, inc=1, device_id=peer, device_id_type=MESH)
    pl.semaphore_wait(barrier, len(peers))

    def amp_rows(g):
        return amp_buf.at[pl.ds(pl.multiple_of(g * rows, rows), rows)]

    def int_rows(b, p):
        return int_buf.at[b, pl.ds(p * cut, cut)]

    def amp_z(d):
        return pltpu.make_async_remote_copy(
            src_ref=amp_rows(grp), dst_ref=amp_rows(grp),
            send_sem=amp_z_send.at[d], recv_sem=amp_z_recv.at[d],
            device_id=at(blk, ((z + d) % planes) * 2 + y), device_id_type=MESH)

    def amp_y(d):
        g = ((z + planes - d) % planes) * 2 + y
        return pltpu.make_async_remote_copy(
            src_ref=amp_rows(g), dst_ref=amp_rows(g),
            send_sem=amp_y_send.at[d], recv_sem=amp_y_recv.at[d],
            device_id=at(blk, z * 2 + 1 - y), device_id_type=MESH)

    def int_x(d, p):
        return pltpu.make_async_remote_copy(
            src_ref=ints_ref.at[pl.ds(p * cut, cut)], dst_ref=int_rows(blk, p),
            send_sem=int_x_send.at[d, p], recv_sem=int_x_recv.at[d, p],
            device_id=at(((x + d) % chips) * 2 + core, grp), device_id_type=MESH)

    def int_c(d, p):
        b = ((x + chips - d) % chips) * 2 + core
        src = ints_ref.at[pl.ds(p * cut, cut)] if d == 0 else int_rows(b, p)
        return pltpu.make_async_remote_copy(
            src_ref=src, dst_ref=int_rows(b, p),
            send_sem=int_c_send.at[d, p], recv_sem=int_c_recv.at[d, p],
            device_id=at(x * 2 + 1 - core, grp), device_id_type=MESH)

    amp_y(0).start()
    for d in range(1, planes):
        amp_z(d).start()
    for p in range(pieces):
        for d in range(1, chips):
            int_x(d, p).start()
    for p in range(pieces):
        int_c(0, p).start()
    own_copy = pltpu.make_async_copy(ints_ref, int_buf.at[blk], local_sem)
    own_copy.start()

    dom = dom_ref[:, pl.ds(pl.multiple_of(blk * group, group), group)]
    own = owner_ref[:, pl.ds(pl.multiple_of(blk * group, group), group)] - blk * group
    hit = jnp.max((dom == target).astype(F32), axis=0, keepdims=True)
    keep = jnp.zeros(dom.shape, F32)
    for c in range(nvb):
        keep = jnp.where(dom == c, (coupling_ref[c, target] > 0).astype(F32), keep)
    code = keep * hit * (dom.astype(F32) + 1.0)
    j_slot = lax.broadcasted_iota(jnp.int32, (group, group * width), 1) // width
    spread = (j_slot == lax.broadcasted_iota(jnp.int32, (group, group * width), 0)).astype(F32)
    by_row = jnp.dot(code.astype(BF16), spread.astype(BF16), preferred_element_type=F32)
    j_k = lax.broadcasted_iota(jnp.int32, (width, group * width), 1) % width
    pick = j_k == lax.broadcasted_iota(jnp.int32, (width, group * width), 0)
    code_row = jnp.sum(jnp.where(pick, by_row, 0.0), axis=0, keepdims=True)
    diag = lax.broadcasted_iota(jnp.int32, (group, group), 0) == lax.broadcasted_iota(
        jnp.int32, (group, group), 1)
    own_col = jnp.sum(jnp.where(diag, own.astype(F32), 0.0), axis=1, keepdims=True)
    code_buf[...] = jnp.where(own_col == j_slot.astype(F32), code_row, 0.0)

    steps = max(planes, (chips - 1) * pieces + 1)
    arrivals = [(d, p) for p in range(pieces) for d in range(1, chips)]
    for s in range(1, steps):
        if s < planes:
            amp_z(s).wait_recv()
            amp_y(s).start()
        if s - 1 < len(arrivals) and s < planes:
            d, p = arrivals[s - 1]
            int_x(d, p).wait_recv()
            int_c(d, p).start()
    done = min(planes - 1, len(arrivals))
    for d in range(planes):
        amp_y(d).wait_recv()

    def build(c, _):
        sel = (code_buf[...] == (c + 1).astype(F32)).astype(F32).astype(BF16)
        tile_buf[c] = jnp.dot(sel, amp_buf[...], preferred_element_type=F32).astype(BF16)
        return 0

    if nvb <= 4:
        for c in range(nvb):
            build(jnp.int32(c), 0)
    else:
        lax.fori_loop(0, nvb, build, 0)

    own_copy.wait()
    out_ref[...] = jnp.dot(tile_buf[blk], int_buf[blk], preferred_element_type=F32)
    sib = x * 2 + 1 - core
    for p in range(pieces):
        int_c(0, p).wait_recv()
    out_ref[...] += jnp.dot(tile_buf[sib], int_buf[sib], preferred_element_type=F32)
    for d, p in arrivals[done:]:
        int_x(d, p).wait_recv()
        int_c(d, p).start()
    for p in range(pieces):
        for d in range(1, chips):
            b = ((x + chips - d) % chips) * 2
            span = pl.ds(p * cut, cut)
            part = jnp.dot(tile_buf[b + core, :, span], int_buf[b + core, span], preferred_element_type=F32)
            int_c(d, p).wait_recv()
            o = b + 1 - core
            part += jnp.dot(tile_buf[o, :, span], int_buf[o, span], preferred_element_type=F32)
            out_ref[...] += part

    for d in range(planes):
        amp_y(d).wait_send()
        if d > 0:
            amp_z(d).wait_send()
    for p in range(pieces):
        for d in range(chips):
            int_c(d, p).wait_send()
            if d > 0:
                int_x(d, p).wait_send()


def solution(mesh):
    n_blk, n_grp = mesh.shape["blk"], mesh.shape["grp"]

    def on_device(amps, domains, owner, coupling, integrals):
        slots, width, depth = amps.shape
        cols = integrals.shape[1]
        group = slots * n_grp
        pieces = 4
        chips, planes = n_blk // 2, n_grp // 2
        dma = pltpu.SemaphoreType.DMA
        vmem = pl.BlockSpec(memory_space=pltpu.VMEM)
        return pl.pallas_call(
            functools.partial(kernel, n_blk, n_grp, pieces),
            out_shape=jax.ShapeDtypeStruct((group, cols), F32),
            in_specs=[vmem, vmem, vmem, pl.BlockSpec(memory_space=pltpu.SMEM), pl.BlockSpec(memory_space=pl.ANY)],
            out_specs=vmem,
            scratch_shapes=[
                pltpu.VMEM((group * width, depth), BF16),
                pltpu.VMEM((n_blk, depth, cols), BF16),
                pltpu.VMEM((n_blk, group, depth), BF16),
                pltpu.VMEM((group, group * width), F32),
                dma((planes,)), dma((planes,)), dma((planes,)), dma((planes,)),
                dma((chips, pieces)), dma((chips, pieces)), dma((chips, pieces)), dma((chips, pieces)),
                dma(()),
            ],
            compiler_params=pltpu.CompilerParams(
                collective_id=0, has_side_effects=True, vmem_limit_bytes=40 * 1024 * 1024),
        )(amps, domains.T, owner.reshape(1, -1), coupling, integrals)

    return jax.shard_map(
        on_device,
        mesh=mesh,
        in_specs=(P(("blk", "grp"), None, None), P(), P(), P(), P("blk", "grp")),
        out_specs=P("blk", "grp"),
        check_vma=False,
    )
```

time: 56.4 us -> 23.8 us (0.42)
  blocking collectives: 33.3 us -> 0 us
  Pallas kernels: 0 us -> 18.8 us
  between operations: 13.5 us -> 0.01 us
  matrix products: 5.44 us -> 0 us
  local copies, waits for them, and re-layouts: 2.3 us -> 4.56 us
  other arithmetic: 0.98 us -> 0 us
  waiting for transfers between devices: 0.73 us -> 0 us
    all_gather x1 -> x0, blocking collectives: 33.3 us -> none  [on_device(): group_amps = lax.all_gather(amps, 'grp', axis=0, tiled=True)]
    pallas_call x0 -> x1, Pallas kernels: none -> 18.8 us  [on_device(): pl.pallas_call(functools.partial(kernel, n_blk, n_grp, pieces), out_shape...]
    dot_general x3 -> x0, matrix products: 5.44 us -> none  [the longest x1 2.37 us: on_device(): jnp.dot(tile_full, lax.all_gather(integrals, 'blk', axis=0, tiled=True),...]
    unnamed x4 -> x11, local copies, waits for them, and re-layouts: 0.63 us -> 4.56 us
    gather x2 -> x0, local copies, waits for them, and re-layouts: 1.54 us -> none  [on_device(): jnp.take(flat_amps, local_slots, axis=0)]
    and x1 -> x0, other arithmetic: 0.77 us -> none  [on_device(): jnp.take(flat_amps, local_slots, axis=0)]
    unnamed x1 -> x0, waiting for transfers between devices: 0.71 us -> none
  transfers between devices with their start and end apart: 1 -> 0, of which waited for: 0 -> 0; matrix products, arithmetic and copies ran while one was open for 11% -> 0% of each run, Pallas kernels for 0% -> 0%
where the time goes in v1:
time: 23.8 us; the launch traced here: 23.4 us
  Pallas kernels  18.8 us (79%)
  local copies, waits for them, and re-layouts  4.56 us (19%)
    pallas_call x1, Pallas kernels, on_device(): pl.pallas_call(functools.partial(kernel, n_blk, n_grp, pieces), out_shape...  18.8 us
    unnamed x11, local copies, waits for them, and re-layouts  4.56 us

profile of v1, /device:TPU:0, one launch (start us, length us, event | category | flops | bytes accessed | tf_op | source)
XLA Modules:
  0.0 23.4 jit_solution(5352290929498572437)
XLA Ops:
  0.0 0.0 copy-start.4
  0.0 0.7 %copy-done.4 = s32[4,4]{1,0:T(4,128)S(1)} copy-done((s32[4,4]{1,0:T(4,128)S(1)}, s32[4,4]{1,0:T(4,128)}, u32[]{:S(2)}) %copy-start.4) | copy-done | bytes 88
  0.7 0.0 copy-start
  0.7 0.9 %copy-done = bf16[512,256]{1,0:T(8,128)(2,1)S(1)} copy-done((bf16[512,256]{1,0:T(8,128)(2,1)S(1)}, bf16[512,256]{1,0:T(8,128)(2,1)}, u32[]{:S(2)}) %copy-start) | copy-done | bytes 262168
  1.6 0.0 copy-start.1
  1.6 0.8 %copy-done.1 = bf16[32,2,512]{2,1,0:T(2,128)(2,1)S(1)} copy-done((bf16[32,2,512]{2,1,0:T(2,128)(2,1)S(1)}, bf16[32,2,512]{2,1,0:T(2,128)(2,1)}, u32[]{:S(2)}) %copy-start.1) | copy-done | bytes 65560
  2.5 0.0 copy-start.2
  2.5 0.7 %copy-done.2 = s32[1024,2]{0,1:T(2,128)S(1)} copy-done((s32[1024,2]{0,1:T(2,128)S(1)}, s32[1024,2]{0,1:T(2,128)}, u32[]{:S(2)}) %copy-start.2) | copy-done | bytes 8216
  3.2 0.0 copy-start.3
  3.2 0.7 %copy-done.3 = s32[1024]{0:T(1024)S(1)} copy-done((s32[1024]{0:T(1024)S(1)}, s32[1024]{0:T(1024)}, u32[]{:S(2)}) %copy-start.3) | copy-done | bytes 4120
  3.9 18.8 %shard_map.55 = f32[256,256]{1,0:T(8,128)S(1)} custom-call(bf16[32,2,512]{2,1,0:T(2,128)(2,1)S(1)} %copy-done.1, s32[2,1024]{1,0:T(2,128)S(1)} %bitcast.2, s32[1,1024]{1,0:T(1,128)S(1)} %bitcast.3, s32[4,4]{1,0:T(4,128)S(1)} %copy-done.4, bf16[512,256]{1,0:T(8,128)(2,1)S(1)} %copy-done), custom_call_target="tpu_custom_call" | custom-call | tf_op jit(solution)/shard_map/pallas_call | solution.py:177
  22.7 0.7 %copy.7 = f32[256,256]{1,0:T(8,128)} copy(f32[256,256]{1,0:T(8,128)S(1)} %shard_map.55) | data formatting | bytes 524288
Async XLA Ops:
  0.0 0.7 %copy-start.4 = (s32[4,4]{1,0:T(4,128)S(1)}, s32[4,4]{1,0:T(4,128)}, u32[]{:S(2)}) copy-start(s32[4,4]{1,0:T(4,128)} %coupling_ref.1) | copy-start | bytes 196
  0.7 0.9 %copy-start = (bf16[512,256]{1,0:T(8,128)(2,1)S(1)}, bf16[512,256]{1,0:T(8,128)(2,1)}, u32[]{:S(2)}) copy-start(bf16[512,256]{1,0:T(8,128)(2,1)} %ints_ref.1) | copy-start | bytes 786436
  1.6 0.8 %copy-start.1 = (bf16[32,2,512]{2,1,0:T(2,128)(2,1)S(1)}, bf16[32,2,512]{2,1,0:T(2,128)(2,1)}, u32[]{:S(2)}) copy-start(bf16[32,2,512]{2,1,0:T(2,128)(2,1)} %amps_ref.1) | copy-start | bytes 196612
  2.5 0.7 %copy-start.2 = (s32[1024,2]{0,1:T(2,128)S(1)}, s32[1024,2]{0,1:T(2,128)}, u32[]{:S(2)}) copy-start(s32[1024,2]{0,1:T(2,128)} %param.6) | copy-start | bytes 24580
  3.2 0.7 %copy-start.3 = (s32[1024]{0:T(1024)S(1)}, s32[1024]{0:T(1024)}, u32[]{:S(2)}) copy-start(s32[1024]{0:T(1024)} %param.7) | copy-start | bytes 12292

commit v2 on v1

--- a/solution.py
+++ b/solution.py
@@ -14,10 +14,10 @@
 
 def kernel(
     n_blk, n_grp, pieces,
-    amps_ref, dom_ref, owner_ref, coupling_ref, ints_ref, out_ref,
-    amp_buf, int_buf, tile_buf, code_buf,
+    amps_hbm, dom_hbm, owner_hbm, coupling_hbm, ints_ref, out_ref,
+    amps_ref, dom_ref, owner_ref, coupling_ref, load_sem, amp_buf, int_buf, tile_buf, code_buf,
     amp_z_send, amp_z_recv, amp_y_send, amp_y_recv,
-    int_x_send, int_x_recv, int_c_send, int_c_recv, local_sem,
+    int_x_send, int_x_recv, int_c_send, int_c_recv, local_sem, ready,
 ):
     chips, planes = n_blk // 2, n_grp // 2
     blk, grp = lax.axis_index("blk"), lax.axis_index("grp")
@@ -34,17 +34,29 @@
     def at(b, g):
         return (b, g)
 
-    mine = amp_buf.at[pl.ds(pl.multiple_of(grp * rows, rows), rows)]
-    mine[...] = amps_ref[...].astype(F32).reshape(rows, depth).astype(BF16)
-
-    peers = [at(blk, ((z + d) % planes) * 2 + y) for d in range(1, planes)]
-    peers.append(at(blk, z * 2 + 1 - y))
-    peers += [at(((x + d) % chips) * 2 + core, grp) for d in range(1, chips)]
-    peers.append(at(x * 2 + 1 - core, grp))
     barrier = pltpu.get_barrier_semaphore()
-    for peer in peers:
-        pl.semaphore_signal(barrier, inc=1, device_id=peer, device_id_type=MESH)
-    pl.semaphore_wait(barrier, len(peers))
+
+    def greet(b, g):
+        pl.semaphore_signal(barrier, inc=1, device_id=at(b, g), device_id_type=MESH)
+
+    for d in range(1, chips):
+        greet(((x + d) % chips) * 2 + core, grp)
+    greet(x * 2 + 1 - core, grp)
+    greet(blk, z * 2 + 1 - y)
+    pl.when(z > 0)(lambda: greet(blk, grp - 2))
+    pl.when(z < planes - 1)(lambda: greet(blk, grp + 2))
+
+    loads = [
+        pltpu.make_async_copy(src, dst, load_sem.at[i])
+        for i, (src, dst) in enumerate((
+            (amps_hbm, amps_ref), (dom_hbm, dom_ref), (owner_hbm, owner_ref), (coupling_hbm, coupling_ref)))
+    ]
+    for load in loads:
+        load.start()
+    own_copy = pltpu.make_async_copy(ints_ref, int_buf.at[blk], local_sem)
+    own_copy.start()
+    at_edge = jnp.where((z == 0) | (z == planes - 1), 1, 0)
+    pl.semaphore_wait(barrier, chips + 3 - at_edge)
 
     def amp_rows(g):
         return amp_buf.at[pl.ds(pl.multiple_of(g * rows, rows), rows)]
@@ -52,18 +64,21 @@
     def int_rows(b, p):
         return int_buf.at[b, pl.ds(p * cut, cut)]
 
-    def amp_z(d):
-        return pltpu.make_async_remote_copy(
-            src_ref=amp_rows(grp), dst_ref=amp_rows(grp),
-            send_sem=amp_z_send.at[d], recv_sem=amp_z_recv.at[d],
-            device_id=at(blk, ((z + d) % planes) * 2 + y), device_id_type=MESH)
-
-    def amp_y(d):
-        g = ((z + planes - d) % planes) * 2 + y
-        return pltpu.make_async_remote_copy(
-            src_ref=amp_rows(g), dst_ref=amp_rows(g),
-            send_sem=amp_y_send.at[d], recv_sem=amp_y_recv.at[d],
+    def amp_z(src, dst):
+        return pltpu.make_async_remote_copy(
+            src_ref=amp_rows(src * 2 + y), dst_ref=amp_rows(src * 2 + y),
+            send_sem=amp_z_send.at[dst], recv_sem=amp_z_recv.at[src],
+            device_id=at(blk, dst * 2 + y), device_id_type=MESH)
+
+    def amp_y(src):
+        return pltpu.make_async_remote_copy(
+            src_ref=amp_rows(src * 2 + y), dst_ref=amp_rows(src * 2 + y),
+            send_sem=amp_y_send.at[src], recv_sem=amp_y_recv.at[src],
             device_id=at(blk, z * 2 + 1 - y), device_id_type=MESH)
+
+    def both_sides(d, do):
+        pl.when(z >= d)(lambda: do(z - d, 1))
+        pl.when(z < planes - d)(lambda: do(z + d, -1))
 
     def int_x(d, p):
         return pltpu.make_async_remote_copy(
@@ -79,17 +94,32 @@
             send_sem=int_c_send.at[d, p], recv_sem=int_c_recv.at[d, p],
             device_id=at(x * 2 + 1 - core, grp), device_id_type=MESH)
 
-    amp_y(0).start()
-    for d in range(1, planes):
-        amp_z(d).start()
     for p in range(pieces):
         for d in range(1, chips):
             int_x(d, p).start()
+    loads[0].wait()
+    amp_rows(grp)[...] = amps_ref[...].astype(F32).reshape(rows, depth).astype(BF16)
+    both_sides(1, lambda to, _: amp_z(z, to).start())
+    amp_y(z).start()
+
+    def tell(other, step):
+        def say():
+            pl.semaphore_signal(ready.at[other], inc=1, device_id=at(blk, (z + step) * 2 + y), device_id_type=MESH)
+        pl.when((z + step >= 0) & (z + step < planes))(say)
+
+    def heard(other, step):
+        pl.semaphore_wait(ready.at[other], 1)
+        tell(other, step)
+        amp_z(z, other).start()
+
+    both_sides(1, tell)
+    for d in range(2, planes):
+        both_sides(d, heard)
     for p in range(pieces):
         int_c(0, p).start()
-    own_copy = pltpu.make_async_copy(ints_ref, int_buf.at[blk], local_sem)
-    own_copy.start()
-
+
+    for load in loads[1:]:
+        load.wait()
     dom = dom_ref[:, pl.ds(pl.multiple_of(blk * group, group), group)]
     own = owner_ref[:, pl.ds(pl.multiple_of(blk * group, group), group)] - blk * group
     hit = jnp.max((dom == target).astype(F32), axis=0, keepdims=True)
@@ -108,19 +138,24 @@
     own_col = jnp.sum(jnp.where(diag, own.astype(F32), 0.0), axis=1, keepdims=True)
     code_buf[...] = jnp.where(own_col == j_slot.astype(F32), code_row, 0.0)
 
-    steps = max(planes, (chips - 1) * pieces + 1)
     arrivals = [(d, p) for p in range(pieces) for d in range(1, chips)]
-    for s in range(1, steps):
-        if s < planes:
-            amp_z(s).wait_recv()
-            amp_y(s).start()
-        if s - 1 < len(arrivals) and s < planes:
-            d, p = arrivals[s - 1]
+
+    def pass_int(some):
+        for d, p in some:
             int_x(d, p).wait_recv()
             int_c(d, p).start()
-    done = min(planes - 1, len(arrivals))
-    for d in range(planes):
-        amp_y(d).wait_recv()
+
+    def pass_amp(src, _):
+        amp_z(src, z).wait_recv()
+        amp_y(src).start()
+
+    share = len(arrivals) // (2 * planes)
+    for d in range(1, planes):
+        both_sides(d, pass_amp)
+        pass_int(arrivals[(d - 1) * share:d * share])
+    done = (planes - 1) * share
+    for src in range(planes):
+        amp_y(src).wait_recv()
 
     def build(c, _):
         sel = (code_buf[...] == (c + 1).astype(F32)).astype(F32).astype(BF16)
@@ -139,9 +174,7 @@
     for p in range(pieces):
         int_c(0, p).wait_recv()
     out_ref[...] += jnp.dot(tile_buf[sib], int_buf[sib], preferred_element_type=F32)
-    for d, p in arrivals[done:]:
-        int_x(d, p).wait_recv()
-        int_c(d, p).start()
+    pass_int(arrivals[done:])
     for p in range(pieces):
         for d in range(1, chips):
             b = ((x + chips - d) % chips) * 2
@@ -155,7 +188,7 @@
     for d in range(planes):
         amp_y(d).wait_send()
         if d > 0:
-            amp_z(d).wait_send()
+            both_sides(d, lambda to, _: amp_z(z, to).wait_send())
     for p in range(pieces):
         for d in range(chips):
             int_c(d, p).wait_send()
@@ -170,27 +203,32 @@
         slots, width, depth = amps.shape
         cols = integrals.shape[1]
         group = slots * n_grp
-        pieces = 4
+        pieces = 8
         chips, planes = n_blk // 2, n_grp // 2
         dma = pltpu.SemaphoreType.DMA
         vmem = pl.BlockSpec(memory_space=pltpu.VMEM)
         return pl.pallas_call(
             functools.partial(kernel, n_blk, n_grp, pieces),
             out_shape=jax.ShapeDtypeStruct((group, cols), F32),
-            in_specs=[vmem, vmem, vmem, pl.BlockSpec(memory_space=pltpu.SMEM), pl.BlockSpec(memory_space=pl.ANY)],
+            in_specs=[pl.BlockSpec(memory_space=pltpu.HBM)] * 5,
             out_specs=vmem,
             scratch_shapes=[
+                pltpu.VMEM(amps.shape, BF16),
+                pltpu.VMEM((width, domains.shape[0]), jnp.int32),
+                pltpu.VMEM((1, owner.shape[0]), jnp.int32),
+                pltpu.SMEM(coupling.shape, jnp.int32),
+                dma((4,)),
                 pltpu.VMEM((group * width, depth), BF16),
                 pltpu.VMEM((n_blk, depth, cols), BF16),
                 pltpu.VMEM((n_blk, group, depth), BF16),
                 pltpu.VMEM((group, group * width), F32),
                 dma((planes,)), dma((planes,)), dma((planes,)), dma((planes,)),
                 dma((chips, pieces)), dma((chips, pieces)), dma((chips, pieces)), dma((chips, pieces)),
-                dma(()),
+                dma(()), pltpu.SemaphoreType.REGULAR((planes,)),
             ],
             compiler_params=pltpu.CompilerParams(
-                collective_id=0, has_side_effects=True, vmem_limit_bytes=40 * 1024 * 1024),
-        )(amps, domains.T, owner.reshape(1, -1), coupling, integrals)
+                collective_id=0, has_side_effects=True, vmem_limit_bytes=48 * 1024 * 1024),
+        )(*(pltpu.with_memory_space_constraint(a, pltpu.HBM) for a in (amps, domains.T, owner.reshape(1, -1), coupling, integrals)))
 
     return jax.shard_map(
         on_device,

time: 23.8 us -> 21.3 us (0.89)
  local copies, waits for them, and re-layouts: 4.56 us -> 0.71 us
  Pallas kernels: 18.8 us -> 20.2 us
    unnamed x11 -> x1, local copies, waits for them, and re-layouts: 4.56 us -> 0.71 us
    pallas_call x1, Pallas kernels: 18.8 us -> 20.2 us  [on_device(): pl.pallas_call(functools.partial(kernel, n_blk, n_grp, pieces), out_shape...]
where the time goes in v2:
time: 21.3 us; the launch traced here: 21 us
  Pallas kernels  20.2 us (95%)
  local copies, waits for them, and re-layouts  0.71 us (3%)
    pallas_call x1, Pallas kernels, on_device(): pl.pallas_call(functools.partial(kernel, n_blk, n_grp, pieces), out_shape...  20.2 us
    unnamed x1, local copies, waits for them, and re-layouts  0.71 us

profile of v2, /device:TPU:0, one launch (start us, length us, event | category | flops | bytes accessed | tf_op | source)
XLA Modules:
  0.0 21.0 jit_solution(2515700077296181873)
XLA Ops:
  0.0 20.2 %shard_map.55 = f32[256,256]{1,0:T(8,128)S(1)} custom-call(bf16[32,2,512]{2,1,0:T(2,128)(2,1)} %amps_hbm.1, s32[2,1024]{1,0:T(2,128)} %bitcast.2, s32[1,1024]{1,0:T(1,128)} %bitcast.3, s32[4,4]{1,0:T(4,128)} %coupling_hbm.1, bf16[512,256]{1,0:T(8,128)(2,1)} %ints_ref.1), custom_call_target="tpu_custom_call" | custom-call | tf_op jit(solution)/shard_map/pallas_call | solution.py:210
  20.2 0.7 %copy.7 = f32[256,256]{1,0:T(8,128)} copy(f32[256,256]{1,0:T(8,128)S(1)} %shard_map.55) | data formatting | bytes 524288

commit v3 on v2

--- a/solution.py
+++ b/solution.py
@@ -13,11 +13,11 @@
 
 
 def kernel(
-    n_blk, n_grp, pieces,
+    n_blk, n_grp, pieces, late,
     amps_hbm, dom_hbm, owner_hbm, coupling_hbm, ints_ref, out_ref,
     amps_ref, dom_ref, owner_ref, coupling_ref, load_sem, amp_buf, int_buf, tile_buf, code_buf,
-    amp_z_send, amp_z_recv, amp_y_send, amp_y_recv,
-    int_x_send, int_x_recv, int_c_send, int_c_recv, local_sem, ready,
+    whole_send, whole_recv, other_send, other_recv, cross_send, cross_recv, late_send, late_recv,
+    int_x_send, int_x_recv, int_c_send, int_c_recv, local_sem,
 ):
     chips, planes = n_blk // 2, n_grp // 2
     blk, grp = lax.axis_index("blk"), lax.axis_index("grp")
@@ -64,17 +64,32 @@
     def int_rows(b, p):
         return int_buf.at[b, pl.ds(p * cut, cut)]
 
-    def amp_z(src, dst):
+    early = rows - late
+
+    def copy(g, first, count, send, recv, to):
+        where = amp_buf.at[pl.ds(pl.multiple_of(g * rows + first, 16), count)]
         return pltpu.make_async_remote_copy(
-            src_ref=amp_rows(src * 2 + y), dst_ref=amp_rows(src * 2 + y),
-            send_sem=amp_z_send.at[dst], recv_sem=amp_z_recv.at[src],
-            device_id=at(blk, dst * 2 + y), device_id_type=MESH)
-
-    def amp_y(src):
-        return pltpu.make_async_remote_copy(
-            src_ref=amp_rows(src * 2 + y), dst_ref=amp_rows(src * 2 + y),
-            send_sem=amp_y_send.at[src], recv_sem=amp_y_recv.at[src],
-            device_id=at(blk, z * 2 + 1 - y), device_id_type=MESH)
+            src_ref=where, dst_ref=where, send_sem=send, recv_sem=recv, device_id=to, device_id_type=MESH)
+
+    def whole(src, step, s=None):
+        sem = src if s is None else s
+        return copy(src * 2 + y, 0, rows, whole_send.at[sem], whole_recv.at[src], at(blk, grp + 2 * step))
+
+    def other(src, step, s=None):
+        sem = src if s is None else s
+        return copy(src * 2 + 1 - y, early, late, other_send.at[sem], other_recv.at[src], at(blk, grp + 2 * step))
+
+    def cross(src):
+        return copy(src * 2 + y, 0, early, cross_send.at[src], cross_recv.at[src], at(blk, z * 2 + 1 - y))
+
+    def cross_late(g):
+        return copy(g, early, late, late_send, late_recv, at(blk, z * 2 + 1 - y))
+
+    def up(do):
+        pl.when(z < planes - 1)(do)
+
+    def down(do):
+        pl.when(z > 0)(do)
 
     def both_sides(d, do):
         pl.when(z >= d)(lambda: do(z - d, 1))
@@ -99,24 +114,15 @@
             int_x(d, p).start()
     loads[0].wait()
     amp_rows(grp)[...] = amps_ref[...].astype(F32).reshape(rows, depth).astype(BF16)
-    both_sides(1, lambda to, _: amp_z(z, to).start())
-    amp_y(z).start()
-
-    def tell(other, step):
-        def say():
-            pl.semaphore_signal(ready.at[other], inc=1, device_id=at(blk, (z + step) * 2 + y), device_id_type=MESH)
-        pl.when((z + step >= 0) & (z + step < planes))(say)
-
-    def heard(other, step):
-        pl.semaphore_wait(ready.at[other], 1)
-        tell(other, step)
-        amp_z(z, other).start()
-
-    both_sides(1, tell)
-    for d in range(2, planes):
-        both_sides(d, heard)
+    cross_late(grp).start()
+    up(lambda: whole(z, 1).start())
+    down(lambda: whole(z, -1, planes).start())
+    cross(z).start()
     for p in range(pieces):
         int_c(0, p).start()
+    cross_late(z * 2 + 1 - y).wait_recv()
+    up(lambda: other(z, 1).start())
+    down(lambda: other(z, -1, planes).start())
 
     for load in loads[1:]:
         load.wait()
@@ -124,9 +130,16 @@
     own = owner_ref[:, pl.ds(pl.multiple_of(blk * group, group), group)] - blk * group
     hit = jnp.max((dom == target).astype(F32), axis=0, keepdims=True)
     keep = jnp.zeros(dom.shape, F32)
+    kept = nvb // 2
+    rank = jnp.int32(0)
+    block_of = [jnp.int32(0)] * kept
     for c in range(nvb):
-        keep = jnp.where(dom == c, (coupling_ref[c, target] > 0).astype(F32), keep)
-    code = keep * hit * (dom.astype(F32) + 1.0)
+        on = (coupling_ref[c, target] > 0).astype(jnp.int32)
+        for r in range(kept):
+            block_of[r] += jnp.where((on > 0) & (rank == r), c, 0)
+        rank += on
+        keep = jnp.where(dom == c, (on * rank).astype(F32), keep)
+    code = keep * hit
     j_slot = lax.broadcasted_iota(jnp.int32, (group, group * width), 1) // width
     spread = (j_slot == lax.broadcasted_iota(jnp.int32, (group, group * width), 0)).astype(F32)
     by_row = jnp.dot(code.astype(BF16), spread.astype(BF16), preferred_element_type=F32)
@@ -145,9 +158,13 @@
             int_x(d, p).wait_recv()
             int_c(d, p).start()
 
-    def pass_amp(src, _):
-        amp_z(src, z).wait_recv()
-        amp_y(src).start()
+    def pass_amp(src, step):
+        further = (z + step >= 0) & (z + step < planes)
+        whole(src, step).wait_recv()
+        pl.when(further)(lambda: whole(src, step).start())
+        cross(src).start()
+        other(src, step).wait_recv()
+        pl.when(further)(lambda: other(src, step).start())
 
     share = len(arrivals) // (2 * planes)
     for d in range(1, planes):
@@ -155,40 +172,43 @@
         pass_int(arrivals[(d - 1) * share:d * share])
     done = (planes - 1) * share
     for src in range(planes):
-        amp_y(src).wait_recv()
+        cross(src).wait_recv()
 
     def build(c, _):
         sel = (code_buf[...] == (c + 1).astype(F32)).astype(F32).astype(BF16)
         tile_buf[c] = jnp.dot(sel, amp_buf[...], preferred_element_type=F32).astype(BF16)
         return 0
 
-    if nvb <= 4:
-        for c in range(nvb):
-            build(jnp.int32(c), 0)
+    pass_int(arrivals[done:])
+    if kept <= 4:
+        for r in range(kept):
+            build(jnp.int32(r), 0)
     else:
-        lax.fori_loop(0, nvb, build, 0)
+        lax.fori_loop(0, kept, build, 0)
 
     own_copy.wait()
-    out_ref[...] = jnp.dot(tile_buf[blk], int_buf[blk], preferred_element_type=F32)
-    sib = x * 2 + 1 - core
-    for p in range(pieces):
-        int_c(0, p).wait_recv()
-    out_ref[...] += jnp.dot(tile_buf[sib], int_buf[sib], preferred_element_type=F32)
-    pass_int(arrivals[done:])
-    for p in range(pieces):
-        for d in range(1, chips):
-            b = ((x + chips - d) % chips) * 2
-            span = pl.ds(p * cut, cut)
-            part = jnp.dot(tile_buf[b + core, :, span], int_buf[b + core, span], preferred_element_type=F32)
+    for p in range(pieces):
+        for d in range(chips):
             int_c(d, p).wait_recv()
-            o = b + 1 - core
-            part += jnp.dot(tile_buf[o, :, span], int_buf[o, span], preferred_element_type=F32)
-            out_ref[...] += part
-
-    for d in range(planes):
-        amp_y(d).wait_send()
-        if d > 0:
-            both_sides(d, lambda to, _: amp_z(z, to).wait_send())
+    total = jnp.dot(tile_buf[0], int_buf[block_of[0]], preferred_element_type=F32)
+    for r in range(1, kept):
+        total += jnp.dot(tile_buf[r], int_buf[block_of[r]], preferred_element_type=F32)
+    out_ref[...] = total
+
+    def sent(src, step):
+        further = (z + step >= 0) & (z + step < planes)
+        pl.when(further)(lambda: whole(src, step).wait_send())
+        pl.when(further)(lambda: other(src, step).wait_send())
+
+    cross_late(grp).wait_send()
+    for src in range(planes):
+        cross(src).wait_send()
+    up(lambda: whole(z, 1).wait_send())
+    up(lambda: other(z, 1).wait_send())
+    down(lambda: whole(z, -1, planes).wait_send())
+    down(lambda: other(z, -1, planes).wait_send())
+    for d in range(1, planes):
+        both_sides(d, sent)
     for p in range(pieces):
         for d in range(chips):
             int_c(d, p).wait_send()
@@ -203,12 +223,13 @@
         slots, width, depth = amps.shape
         cols = integrals.shape[1]
         group = slots * n_grp
-        pieces = 8
+        pieces = 4
+        late = slots * width // 2
         chips, planes = n_blk // 2, n_grp // 2
         dma = pltpu.SemaphoreType.DMA
         vmem = pl.BlockSpec(memory_space=pltpu.VMEM)
         return pl.pallas_call(
-            functools.partial(kernel, n_blk, n_grp, pieces),
+            functools.partial(kernel, n_blk, n_grp, pieces, late),
             out_shape=jax.ShapeDtypeStruct((group, cols), F32),
             in_specs=[pl.BlockSpec(memory_space=pltpu.HBM)] * 5,
             out_specs=vmem,
@@ -220,11 +241,12 @@
                 dma((4,)),
                 pltpu.VMEM((group * width, depth), BF16),
                 pltpu.VMEM((n_blk, depth, cols), BF16),
-                pltpu.VMEM((n_blk, group, depth), BF16),
+                pltpu.VMEM((n_blk // 2, group, depth), BF16),
                 pltpu.VMEM((group, group * width), F32),
-                dma((planes,)), dma((planes,)), dma((planes,)), dma((planes,)),
+                dma((planes + 1,)), dma((planes,)), dma((planes + 1,)), dma((planes,)),
+                dma((planes,)), dma((planes,)), dma(()), dma(()),
                 dma((chips, pieces)), dma((chips, pieces)), dma((chips, pieces)), dma((chips, pieces)),
-                dma(()), pltpu.SemaphoreType.REGULAR((planes,)),
+                dma(()),
             ],
             compiler_params=pltpu.CompilerParams(
                 collective_id=0, has_side_effects=True, vmem_limit_bytes=48 * 1024 * 1024),

time: 21.3 us -> 22.1 us (1.038)
  the two profiles are of different devices: /device:TPU:0 before, /device:TPU:1 now
where the time goes in v3:
time: 22.1 us; the launch traced here: 22 us
  Pallas kernels  21.3 us (96%)
  local copies, waits for them, and re-layouts  0.71 us (3%)
    pallas_call x1, Pallas kernels, on_device(): pl.pallas_call(functools.partial(kernel, n_blk, n_grp, pieces, late), out...  21.3 us
    unnamed x1, local copies, waits for them, and re-layouts  0.71 us

profile of v3, /device:TPU:1, one launch (start us, length us, event | category | flops | bytes accessed | tf_op | source)
XLA Modules:
  0.0 22.0 jit_solution(14716398800666189744)
XLA Ops:
  0.0 21.3 %shard_map.55 = f32[256,256]{1,0:T(8,128)S(1)} custom-call(bf16[32,2,512]{2,1,0:T(2,128)(2,1)} %amps_hbm.1, s32[2,1024]{1,0:T(2,128)} %bitcast.2, s32[1,1024]{1,0:T(1,128)} %bitcast.3, s32[4,4]{1,0:T(4,128)} %coupling_hbm.1, bf16[512,256]{1,0:T(8,128)(2,1)} %ints_ref.1), custom_call_target="tpu_custom_call" | custom-call | tf_op jit(solution)/shard_map/pallas_call | solution.py:231
  21.3 0.7 %copy.7 = f32[256,256]{1,0:T(8,128)} copy(f32[256,256]{1,0:T(8,128)S(1)} %shard_map.55) | data formatting | bytes 524288

commit v4 on v2

--- a/solution.py
+++ b/solution.py
@@ -124,9 +124,16 @@
     own = owner_ref[:, pl.ds(pl.multiple_of(blk * group, group), group)] - blk * group
     hit = jnp.max((dom == target).astype(F32), axis=0, keepdims=True)
     keep = jnp.zeros(dom.shape, F32)
+    kept = nvb // 2
+    rank = jnp.int32(0)
+    block_of = [jnp.int32(0)] * kept
     for c in range(nvb):
-        keep = jnp.where(dom == c, (coupling_ref[c, target] > 0).astype(F32), keep)
-    code = keep * hit * (dom.astype(F32) + 1.0)
+        on = (coupling_ref[c, target] > 0).astype(jnp.int32)
+        for r in range(kept):
+            block_of[r] += jnp.where((on > 0) & (rank == r), c, 0)
+        rank += on
+        keep = jnp.where(dom == c, (on * rank).astype(F32), keep)
+    code = keep * hit
     j_slot = lax.broadcasted_iota(jnp.int32, (group, group * width), 1) // width
     spread = (j_slot == lax.broadcasted_iota(jnp.int32, (group, group * width), 0)).astype(F32)
     by_row = jnp.dot(code.astype(BF16), spread.astype(BF16), preferred_element_type=F32)
@@ -149,11 +156,9 @@
         amp_z(src, z).wait_recv()
         amp_y(src).start()
 
-    share = len(arrivals) // (2 * planes)
     for d in range(1, planes):
         both_sides(d, pass_amp)
-        pass_int(arrivals[(d - 1) * share:d * share])
-    done = (planes - 1) * share
+    pass_int(arrivals)
     for src in range(planes):
         amp_y(src).wait_recv()
 
@@ -162,28 +167,20 @@
         tile_buf[c] = jnp.dot(sel, amp_buf[...], preferred_element_type=F32).astype(BF16)
         return 0
 
-    if nvb <= 4:
-        for c in range(nvb):
-            build(jnp.int32(c), 0)
+    if kept <= 4:
+        for r in range(kept):
+            build(jnp.int32(r), 0)
     else:
-        lax.fori_loop(0, nvb, build, 0)
+        lax.fori_loop(0, kept, build, 0)
 
     own_copy.wait()
-    out_ref[...] = jnp.dot(tile_buf[blk], int_buf[blk], preferred_element_type=F32)
-    sib = x * 2 + 1 - core
-    for p in range(pieces):
-        int_c(0, p).wait_recv()
-    out_ref[...] += jnp.dot(tile_buf[sib], int_buf[sib], preferred_element_type=F32)
-    pass_int(arrivals[done:])
-    for p in range(pieces):
-        for d in range(1, chips):
-            b = ((x + chips - d) % chips) * 2
-            span = pl.ds(p * cut, cut)
-            part = jnp.dot(tile_buf[b + core, :, span], int_buf[b + core, span], preferred_element_type=F32)
+    for p in range(pieces):
+        for d in range(chips):
             int_c(d, p).wait_recv()
-            o = b + 1 - core
-            part += jnp.dot(tile_buf[o, :, span], int_buf[o, span], preferred_element_type=F32)
-            out_ref[...] += part
+    total = jnp.dot(tile_buf[0], int_buf[block_of[0]], preferred_element_type=F32)
+    for r in range(1, kept):
+        total += jnp.dot(tile_buf[r], int_buf[block_of[r]], preferred_element_type=F32)
+    out_ref[...] = total
 
     for d in range(planes):
         amp_y(d).wait_send()
@@ -203,7 +200,7 @@
         slots, width, depth = amps.shape
         cols = integrals.shape[1]
         group = slots * n_grp
-        pieces = 8
+        pieces = 4
         chips, planes = n_blk // 2, n_grp // 2
         dma = pltpu.SemaphoreType.DMA
         vmem = pl.BlockSpec(memory_space=pltpu.VMEM)
@@ -220,7 +217,7 @@
                 dma((4,)),
                 pltpu.VMEM((group * width, depth), BF16),
                 pltpu.VMEM((n_blk, depth, cols), BF16),
-                pltpu.VMEM((n_blk, group, depth), BF16),
+                pltpu.VMEM((n_blk // 2, group, depth), BF16),
                 pltpu.VMEM((group, group * width), F32),
                 dma((planes,)), dma((planes,)), dma((planes,)), dma((planes,)),
                 dma((chips, pieces)), dma((chips, pieces)), dma((chips, pieces)), dma((chips, pieces)),

time: 21.3 us -> 18.5 us (0.87)
  Pallas kernels: 20.2 us -> 17.7 us
    pallas_call x1, Pallas kernels: 20.2 us -> 17.7 us  [on_device(): pl.pallas_call(functools.partial(kernel, n_blk, n_grp, pieces), out_shape...]
where the time goes in v4:
time: 18.5 us; the launch traced here: 18.4 us
  Pallas kernels  17.7 us (96%)
  local copies, waits for them, and re-layouts  0.71 us (4%)
    pallas_call x1, Pallas kernels, on_device(): pl.pallas_call(functools.partial(kernel, n_blk, n_grp, pieces), out_shape...  17.7 us
    unnamed x1, local copies, waits for them, and re-layouts  0.71 us

profile of v4, /device:TPU:0, one launch (start us, length us, event | category | flops | bytes accessed | tf_op | source)
XLA Modules:
  0.0 18.4 jit_solution(11498704699576837288)
XLA Ops:
  0.0 17.7 %shard_map.55 = f32[256,256]{1,0:T(8,128)S(1)} custom-call(bf16[32,2,512]{2,1,0:T(2,128)(2,1)} %amps_hbm.1, s32[2,1024]{1,0:T(2,128)} %bitcast.2, s32[1,1024]{1,0:T(1,128)} %bitcast.3, s32[4,4]{1,0:T(4,128)} %coupling_hbm.1, bf16[512,256]{1,0:T(8,128)(2,1)} %ints_ref.1), custom_call_target="tpu_custom_call" | custom-call | tf_op jit(solution)/shard_map/pallas_call | solution.py:207
  17.7 0.7 %copy.7 = f32[256,256]{1,0:T(8,128)} copy(f32[256,256]{1,0:T(8,128)S(1)} %shard_map.55) | data formatting | bytes 524288

commit v5 on v4

--- a/solution.py
+++ b/solution.py
@@ -97,24 +97,22 @@
     for p in range(pieces):
         for d in range(1, chips):
             int_x(d, p).start()
+    def tell(other, step):
+        def say():
+            pl.semaphore_signal(ready.at[other], inc=1, device_id=at(blk, (z + step) * 2 + y), device_id_type=MESH)
+        pl.when((z + step >= 0) & (z + step < planes))(say)
+
+    def heard(other, step):
+        pl.semaphore_wait(ready.at[other], 1)
+        tell(other, step)
+        amp_z(z, other).start()
+
+    both_sides(1, tell)
     loads[0].wait()
     amp_rows(grp)[...] = amps_ref[...].astype(F32).reshape(rows, depth).astype(BF16)
     both_sides(1, lambda to, _: amp_z(z, to).start())
     amp_y(z).start()
 
-    def tell(other, step):
-        def say():
-            pl.semaphore_signal(ready.at[other], inc=1, device_id=at(blk, (z + step) * 2 + y), device_id_type=MESH)
-        pl.when((z + step >= 0) & (z + step < planes))(say)
-
-    def heard(other, step):
-        pl.semaphore_wait(ready.at[other], 1)
-        tell(other, step)
-        amp_z(z, other).start()
-
-    both_sides(1, tell)
-    for d in range(2, planes):
-        both_sides(d, heard)
     for p in range(pieces):
         int_c(0, p).start()
 
@@ -156,8 +154,10 @@
         amp_z(src, z).wait_recv()
         amp_y(src).start()
 
-    for d in range(1, planes):
-        both_sides(d, pass_amp)
+    for d in range(2, planes):
+        both_sides(d, heard)
+        both_sides(d - 1, pass_amp)
+    both_sides(planes - 1, pass_amp)
     pass_int(arrivals)
     for src in range(planes):
         amp_y(src).wait_recv()

time: 18.5 us -> 18 us (0.973)
  Pallas kernels: 17.7 us -> 17.1 us
    pallas_call x1, Pallas kernels: 17.7 us -> 17.1 us  [on_device(): pl.pallas_call(functools.partial(kernel, n_blk, n_grp, pieces), out_shape...]
where the time goes in v5:
time: 18 us; the launch traced here: 17.8 us
  Pallas kernels  17.1 us (95%)
  local copies, waits for them, and re-layouts  0.71 us (4%)
    pallas_call x1, Pallas kernels, on_device(): pl.pallas_call(functools.partial(kernel, n_blk, n_grp, pieces), out_shape...  17.1 us
    unnamed x1, local copies, waits for them, and re-layouts  0.71 us

profile of v5, /device:TPU:0, one launch (start us, length us, event | category | flops | bytes accessed | tf_op | source)
XLA Modules:
  0.0 17.8 jit_solution(2020922010136162490)
XLA Ops:
  0.0 17.1 %shard_map.55 = f32[256,256]{1,0:T(8,128)S(1)} custom-call(bf16[32,2,512]{2,1,0:T(2,128)(2,1)} %amps_hbm.1, s32[2,1024]{1,0:T(2,128)} %bitcast.2, s32[1,1024]{1,0:T(1,128)} %bitcast.3, s32[4,4]{1,0:T(4,128)} %coupling_hbm.1, bf16[512,256]{1,0:T(8,128)(2,1)} %ints_ref.1), custom_call_target="tpu_custom_call" | custom-call | tf_op jit(solution)/shard_map/pallas_call | solution.py:207
  17.1 0.7 %copy.7 = f32[256,256]{1,0:T(8,128)} copy(f32[256,256]{1,0:T(8,128)S(1)} %shard_map.55) | data formatting | bytes 524288

commit v6 on v5

--- a/solution.py
+++ b/solution.py
@@ -157,8 +157,8 @@
     for d in range(2, planes):
         both_sides(d, heard)
         both_sides(d - 1, pass_amp)
+    pass_int(arrivals)
     both_sides(planes - 1, pass_amp)
-    pass_int(arrivals)
     for src in range(planes):
         amp_y(src).wait_recv()
 

time: 18 us -> 18 us (level)
  no operation moved by 1% of the time
where the time goes in v6:
time: 18 us; the launch traced here: 17.8 us
  Pallas kernels  17.1 us (95%)
  local copies, waits for them, and re-layouts  0.71 us (4%)
    pallas_call x1, Pallas kernels, on_device(): pl.pallas_call(functools.partial(kernel, n_blk, n_grp, pieces), out_shape...  17.1 us
    unnamed x1, local copies, waits for them, and re-layouts  0.71 us

profile of v6, /device:TPU:0, one launch (start us, length us, event | category | flops | bytes accessed | tf_op | source)
XLA Modules:
  0.0 17.8 jit_solution(12428405555581226026)
XLA Ops:
  0.0 17.1 %shard_map.55 = f32[256,256]{1,0:T(8,128)S(1)} custom-call(bf16[32,2,512]{2,1,0:T(2,128)(2,1)} %amps_hbm.1, s32[2,1024]{1,0:T(2,128)} %bitcast.2, s32[1,1024]{1,0:T(1,128)} %bitcast.3, s32[4,4]{1,0:T(4,128)} %coupling_hbm.1, bf16[512,256]{1,0:T(8,128)(2,1)} %ints_ref.1), custom_call_target="tpu_custom_call" | custom-call | tf_op jit(solution)/shard_map/pallas_call | solution.py:207
  17.1 0.7 %copy.7 = f32[256,256]{1,0:T(8,128)} copy(f32[256,256]{1,0:T(8,128)S(1)} %shard_map.55) | data formatting | bytes 524288
